TPU v7x, 1024 devices: a whole 4x8x16 slice. The times are simulated.
1024 devices in a mesh: comp: 2 (over x_hi), row: 32 (over x_lo, y, core), col: 16 (over z).
Axes of the slice: x: 4 (x_hi: 2, x_lo: 2; x = x_hi * 2 + x_lo), y: 8, z: 16, core: 2. Of those that a mesh axis runs over, the one named last changes fastest.
Arguments:
- model_state: float32 [2, 1280, 32, 2048], P('comp', 'row', None, 'col'), may hold values from -6 to 6
- legendre: bfloat16 [32, 1280, 1280], P('row'), may hold values from -0.15625 to 0.15625
- gauss_weight: float32 [1280], P('row'), may hold values from 0.5 to 1.5
- mixing: float32 [32, 32], replicated, may hold values from -1 to 1
- surface: float32 [2, 1280, 2048], P('comp', 'row', 'col'), may hold values from -6 to 6
- sea_count: int32 [2, 1280, 16], P('comp', 'row', 'col'), may hold values from 0 to 128, as said below
- remap_source: int32 [2, 1280, 2048], P('comp', 'row', 'col'), may hold values from 0 to 5119
Outputs:
- new_state: float32 [2, 1280, 32, 2048], P('comp', 'row', None, 'col')
- new_surface: float32 [2, 1280, 2048], P('comp', 'row', 'col')
Inputs may be any that keep to these rules, and one draw needn't show every extreme that they name: `sea_count`: the sea cells of a tile row are its first ones, of 128. `remap_source`: an entry counts row-major within a tile of 40 rows and 128 columns.
All inputs are finite; a program needn't handle non-finite values.
Results may differ from a plain program's by a relative error of at most 0.0043.
Values may be sent and summed in bfloat16 or wider, within the bound.
A program may use at most 32 MiB of HBM per device.

v0:
```python
import jax
import jax.numpy as jnp
from jax import lax
from jax.sharding import PartitionSpec as P

diffusion_rate = 0.2


def padded_2(block, sides, width):
    for axis, dim in sides:
        count = lax.axis_size(axis)
        forward = [(i, i + 1) for i in range(count - 1)]
        backward = [(target, source) for source, target in forward]
        low = lax.ppermute(
            lax.slice_in_dim(block, block.shape[dim] - width, None, axis=dim), axis, forward
        )
        high = lax.ppermute(lax.slice_in_dim(block, 0, width, axis=dim), axis, backward)
        block = jnp.concatenate([low, block, high], axis=dim)
    return block


def swapped(block, axis, stride):
    count = lax.axis_size(axis)
    route = []
    for low in range(count):
        high = low | 1 << stride
        if high != low and high < count:
            route += [(low, high), (high, low)]
    return lax.ppermute(block, axis, route)


def damping_table(row_index, wave_dev, nwave_count):
    global_wave = row_index * wave_dev + jnp.arange(wave_dev, dtype=jnp.int32)
    total_wave = (global_wave[:, None] + jnp.arange(nwave_count, dtype=jnp.int32)[None, :]).astype(
        jnp.float32
    )
    wave_ratio = total_wave * (total_wave + 1.0) / (1279.0 * 1280.0)
    return 1.0 / (1.0 + 20.0 * wave_ratio * wave_ratio)


def laplace_inner(padded):
    centre = padded[1:-1, :, 1:-1]
    return (
        padded[2:, :, 1:-1]
        + padded[:-2, :, 1:-1]
        + padded[1:-1, :, 2:]
        + padded[1:-1, :, :-2]
        - 4.0 * centre
    )


def atmosphere(fields, gauss_weight, legendre):
    weighted = (gauss_weight[None, :, None] * jnp.transpose(fields, (1, 0, 2))).astype(jnp.bfloat16)
    damping = damping_table(lax.axis_index("row"), legendre.shape[0], legendre.shape[2])
    spectral = jnp.einsum(
        "wln,wlc->wnc",
        legendre,
        lax.all_to_all(weighted, "row", split_axis=0, concat_axis=1, tiled=True),
        preferred_element_type=jnp.float32,
    )
    filtered = (damping[:, :, None] * spectral).astype(jnp.bfloat16)
    synthesized = jnp.einsum(
        "wln,wnc->wlc", legendre, filtered, preferred_element_type=jnp.float32
    ).astype(jnp.bfloat16)
    returned = lax.all_to_all(synthesized, "row", split_axis=1, concat_axis=0, tiled=True)
    return jnp.transpose(returned, (1, 0, 2)).astype(jnp.float32)


def advance_ocean(heat_level, mixing, water_mask):
    water_column = water_mask[:, None, :]
    blended_field = heat_level + water_column * jnp.einsum(
        "do,eot->edt", mixing, heat_level, precision=lax.Precision.HIGHEST
    )
    current = blended_field
    for sweep_index in range(2):
        padded = padded_2(water_column * current, (("row", 0), ("col", 2)), 1)
        current = current + diffusion_rate * water_column * laplace_inner(padded)
    return current


def shards(model_state, legendre, gauss_weight, mixing, surface, sea_count, remap_source):
    fields = model_state[0]
    counts = sea_count[0, :, 0]
    water_mask = (jnp.arange(fields.shape[2], dtype=jnp.int32)[None, :] < counts[:, None]).astype(
        jnp.float32
    )
    own_surface = surface[0]
    group_index = lax.axis_index("comp")
    air_result = atmosphere(fields, gauss_weight, legendre)
    sea_result = advance_ocean(fields, mixing, water_mask)
    result = jnp.where(group_index == 0, air_result, sea_result)
    partner = swapped(own_surface, "comp", 0)
    pulled = jnp.take(partner.reshape(-1), remap_source[0].reshape(-1)).reshape(own_surface.shape)
    surface_gap = water_mask * (pulled - own_surface)
    slot_rate = jnp.where(group_index == 0, 0.5, 0.25).astype(jnp.float32)
    ocean_share = jnp.where(group_index == 0, 0.0, 0.3).astype(jnp.float32)
    new_surface = own_surface + slot_rate * surface_gap
    result = result.at[:, 0, :].add(ocean_share * surface_gap)
    return (result[None], new_surface[None])


def solution(mesh):
    in_specs = (
        P("comp", "row", None, "col"),
        P("row", None, None),
        P("row"),
        P(),
        P("comp", "row", "col"),
        P("comp", "row", "col"),
        P("comp", "row", "col"),
    )
    out_specs = (P("comp", "row", None, "col"), P("comp", "row", "col"))
    return jax.shard_map(shards, mesh=mesh, in_specs=in_specs, out_specs=out_specs, check_vma=False)
```

profile of v0, /device:TPU:1, one launch (start us, length us, event | category | flops | bytes accessed | tf_op | source)
XLA Modules:
  0.0 135.7 jit_solution(883167602183431865)
XLA Ops:
  0.6 0.0 copy-start
  0.7 0.9 fusion.45
  1.6 3.0 %broadcast_multiply_fusion.1 = (f32[40,32,128]{2,1,0:T(8,128)S(1)}, f32[40,32,128]{2,1,0:T(8,128)}) fusion(f32[40,128]{1,0:T(8,128)S(1)} %fusion.45, f32[32,32]{1,0:T(8,128)} %param.12, f32[1,40,32,128]{3,2,1,0:T(8,128)} %param.9), kind=kOutput, calls=%fused_computation.48 | convolution fusion | flops 63406080 | bytes 1990656 | tf_op jit(solution)/shard_map/do,eot->edt/dot_general | solution.py:71
  4.5 0.9 copy-done.2
  5.4 16.0 %collective-permute-start = (f32[1,32,128]{2,1,0:T(8,128)S(1)}, f32[1,32,128]{2,1,0:T(8,128)S(1)}, u32[]{:S(2)}, u32[]{:S(2)}) collective-permute-start(f32[1,32,128]{2,1,0:T(8,128)S(1)} %get-tuple-element.23), channel_id=1, source_target_pairs={{16,0},{32,16},{48,32},{64,48},{80,64},{96,80},{112,96},{128,112},... | collective-permute-start | bytes 49160 | tf_op jit(solution)/shard_map/ppermute | solution.py:17
  21.5 1.9 %collective-permute-start.1 = (f32[1,32,128]{2,1,0:T(8,128)S(1)}, f32[1,32,128]{2,1,0:T(8,128)S(1)}, u32[]{:S(2)}, u32[]{:S(2)}) collective-permute-start(f32[1,32,128]{2,1,0:T(8,128)S(1)} %get-tuple-element.22), channel_id=1, source_target_pairs={{0,16},{16,32},{32,48},{48,64},{64,80},{80,96},{96,112},{112,128},... | collective-permute-start | bytes 49160 | tf_op jit(solution)/shard_map/ppermute | solution.py:14
  23.4 1.2 fusion.35
  24.6 0.9 copy.15
  25.5 4.7 %all-to-all-start = ((bf16[32,40,128]{2,1,0:T(8,128)(2,1)}), bf16[32,40,128]{2,1,0:T(8,128)(2,1)}, u32[]{:S(2)}, u32[]{:S(2)}) async-start(bf16[32,40,128]{2,1,0:T(8,128)(2,1)} %copy.15), calls=%async_computation | async-start | bytes 655360 | tf_op jit(solution)/shard_map/all_to_all | solution.py:58
  30.2 1.9 %collective-permute-start.8 = (f32[40,128]{1,0:T(8,128)S(1)}, f32[40,128]{1,0:T(8,128)S(1)}, u32[]{:S(2)}, u32[]{:S(2)}) collective-permute-start(f32[40,128]{1,0:T(8,128)S(1)} %bitcast.79), channel_id=1, source_target_pairs={{0,512},{512,0},{1,513},{513,1},{2,514},{514,2},{3,515},{515,3},{4... | collective-permute-start | bytes 61448 | tf_op jit(solution)/shard_map/ppermute | solution.py:29
  32.1 0.1 fusion.44
  32.2 1.1 pad_maximum_fusion
  33.4 1.3 fusion.50
  34.7 1.5 %copy.19 = f32[42,32,1]{0,1,2:T(8,128)S(1)} copy(f32[42,32,1]{2,1,0:T(8,128)} %get-tuple-element.18) | data formatting | bytes 10752 | tf_op jit(solution)/shard_map/slice | solution.py:17
  36.2 1.3 collective-permute-start.2
  37.5 1.5 %copy.21 = f32[42,32,1]{0,1,2:T(8,128)S(1)} copy(f32[42,32,1]{2,1,0:T(8,128)} %get-tuple-element.19) | data formatting | bytes 10752 | tf_op jit(solution)/shard_map/slice | solution.py:15
  39.0 4.0 %collective-permute-start.3 = (f32[42,32,1]{0,1,2:T(8,128)S(1)}, f32[42,32,1]{0,1,2:T(8,128)S(1)}, u32[]{:S(2)}, u32[]{:S(2)}) collective-permute-start(f32[42,32,1]{0,1,2:T(8,128)S(1)} %copy.21), channel_id=1, source_target_pairs={{0,1},{1,2},{2,3},{3,4},{4,5},{5,6},{6,7},{7,8},{8,9},{9,10},{10,1... | collective-permute-start | bytes 16136 | tf_op jit(solution)/shard_map/ppermute | solution.py:14
  43.0 0.0 collective-permute-done.2
  43.0 1.5 %copy.20 = f32[42,32,1]{2,1,0:T(8,128)} copy(f32[42,32,1]{0,1,2:T(8,128)S(1)} %collective-permute-done.2) | data formatting | bytes 10752 | tf_op jit(solution)/shard_map/ppermute | solution.py:17
  44.6 1.5 %copy.22 = f32[42,32,1]{2,1,0:T(8,128)} copy(f32[42,32,1]{0,1,2:T(8,128)S(1)} %collective-permute-done.3) | data formatting | bytes 10752 | tf_op jit(solution)/shard_map/ppermute | solution.py:14
  46.1 4.2 %broadcast_multiply_fusion = (f32[40,32,128]{2,1,0:T(8,128)S(1)}, f32[40,32,128]{2,1,0:T(8,128)}) fusion(f32[40,128]{1,0:T(8,128)S(1)} %fusion.45, f32[40,32,128]{2,1,0:T(8,128)} %get-tuple-element.25, f32[40,32,128]{2,1,0:T(8,128)} %copy-done.2, f32[1,32,128]{2,1,0:T(8,128)S(1)} %collective-permute-done, f32[1,32,128]{2,1,0:T(8,128)S(1)} %collective-permute-done.1, ...), kind=kLoop, calls=%fused_computation.47 | loop fusion | flops 2621440 | bytes 2705920 | tf_op jit(solution)/shard_map/mul | solution.py:76
  50.3 0.9 copy-done.1
  51.1 2.9 %collective-permute-start.4 = (f32[1,32,128]{2,1,0:T(8,128)S(1)}, f32[1,32,128]{2,1,0:T(8,128)S(1)}, u32[]{:S(2)}, u32[]{:S(2)}) collective-permute-start(f32[1,32,128]{2,1,0:T(8,128)S(1)} %get-tuple-element.21), channel_id=1, source_target_pairs={{16,0},{32,16},{48,32},{64,48},{80,64},{96,80},{112,96},{128,112},... | collective-permute-start | bytes 49160 | tf_op jit(solution)/shard_map/ppermute | solution.py:17
  54.0 3.1 %collective-permute-start.5 = (f32[1,32,128]{2,1,0:T(8,128)S(1)}, f32[1,32,128]{2,1,0:T(8,128)S(1)}, u32[]{:S(2)}, u32[]{:S(2)}) collective-permute-start(f32[1,32,128]{2,1,0:T(8,128)S(1)} %get-tuple-element.20), channel_id=1, source_target_pairs={{0,16},{16,32},{32,48},{48,64},{64,80},{80,96},{96,112},{112,128},... | collective-permute-start | bytes 49160 | tf_op jit(solution)/shard_map/ppermute | solution.py:14
  57.2 3.4 %fusion.13 = bf16[1,1280,128]{1,2,0:T(8,128)(2,1)} fusion(bf16[1,1280,1280]{2,1,0:T(8,128)(2,1)S(1)} %copy-done, bf16[1280,128]{1,0:T(8,128)(2,1)} %bitcast.2, f32[1280]{0:T(1024)S(1)} %add_divide_fusion), kind=kOutput, calls=%fused_computation.8 | convolution fusion | flops 839352320 | bytes 3937280 | tf_op jit(solution)/shard_map/wln,wnc->wlc/dot_general | solution.py:62
  60.6 2.1 %copy.16 = bf16[1,1280,128]{2,0,1:T(2,128)(2,1)} copy(bf16[1,1280,128]{1,2,0:T(8,128)(2,1)} %fusion.13) | data formatting | bytes 655360 | tf_op jit(solution)/shard_map/convert_element_type | solution.py:64
  62.7 0.5 broadcast.229
  63.2 9.1 %reduce.2 = bf16[1280,128]{1,0:T(8,128)(2,1)} reduce(bf16[1280,1,128]{2,1,0:T(2,128)(2,1)} %bitcast.72, bf16[]{:T(256)} %broadcast.229), dimensions={1}, to_apply=%bitcast.64.reduce_sub_computation | reduce | bytes 655362
  72.3 1.8 %reshape.289 = bf16[32,2,2560]{2,1,0:T(2,128)(2,1)} reshape(bf16[1280,128]{1,0:T(8,128)(2,1)} %reduce.2) | data formatting | bytes 655360
  74.1 7.8 %all-to-all-start.1 = ((bf16[32,2,2560]{2,1,0:T(2,128)(2,1)}), bf16[32,2,2560]{2,1,0:T(2,128)(2,1)}, u32[]{:S(2)}, u32[]{:S(2)}) async-start(bf16[32,2,2560]{2,1,0:T(2,128)(2,1)} %reshape.289), calls=%async_computation.1 | async-start | bytes 655360 | tf_op jit(solution)/shard_map/all_to_all | solution.py:65
  81.9 0.0 collective-permute-done.8
  81.9 28.7 %gather_fusion = f32[5120]{0:T(1024)S(1)} fusion(f32[5120]{0:T(1024)S(1)} %bitcast.71, s32[5120]{0:T(1024)S(1)} %broadcast_clamp_fusion), kind=kCustom, calls=%fused_computation | custom fusion | bytes 61440 | tf_op jit(solution)/shard_map/jit(_take)/gather | solution.py:93
  110.6 1.1 pad_maximum_fusion.1
  111.7 1.3 fusion.49
  113.0 1.5 %copy.23 = f32[42,32,1]{0,1,2:T(8,128)S(1)} copy(f32[42,32,1]{2,1,0:T(8,128)} %get-tuple-element.16) | data formatting | bytes 10752 | tf_op jit(solution)/shard_map/slice | solution.py:17
  114.6 1.3 collective-permute-start.6
  115.9 1.5 %copy.25 = f32[42,32,1]{0,1,2:T(8,128)S(1)} copy(f32[42,32,1]{2,1,0:T(8,128)} %get-tuple-element.17) | data formatting | bytes 10752 | tf_op jit(solution)/shard_map/slice | solution.py:15
  117.4 4.2 %collective-permute-start.7 = (f32[42,32,1]{0,1,2:T(8,128)S(1)}, f32[42,32,1]{0,1,2:T(8,128)S(1)}, u32[]{:S(2)}, u32[]{:S(2)}) collective-permute-start(f32[42,32,1]{0,1,2:T(8,128)S(1)} %copy.25), channel_id=1, source_target_pairs={{0,1},{1,2},{2,3},{3,4},{4,5},{5,6},{6,7},{7,8},{8,9},{9,10},{10,1... | collective-permute-start | bytes 16136 | tf_op jit(solution)/shard_map/ppermute | solution.py:14
  121.6 0.7 fusion.43
  122.3 1.5 %copy.24 = f32[42,32,1]{2,1,0:T(8,128)} copy(f32[42,32,1]{0,1,2:T(8,128)S(1)} %collective-permute-done.6) | data formatting | bytes 10752 | tf_op jit(solution)/shard_map/ppermute | solution.py:17
  123.8 1.5 %copy.26 = f32[42,32,1]{2,1,0:T(8,128)} copy(f32[42,32,1]{0,1,2:T(8,128)S(1)} %collective-permute-done.7) | data formatting | bytes 10752 | tf_op jit(solution)/shard_map/ppermute | solution.py:14
  125.3 3.2 %reshape.290 = bf16[1280,1,128]{2,1,0:T(2,128)(2,1)} reshape(bf16[32,2,2560]{2,1,0:T(2,128)(2,1)} %all-to-all-done.1) | data formatting | bytes 655360
  128.5 1.1 copy.17
  129.7 3.4 %fusion.24 = f32[40,32,128]{2,1,0:T(8,128)S(1)} fusion(f32[40,32,128]{2,1,0:T(8,128)} %get-tuple-element.15, f32[42,32,1]{2,1,0:T(8,128)} %copy.26, f32[1,32,128]{2,1,0:T(8,128)S(1)} %collective-permute-done.4, f32[40,32,128]{2,1,0:T(8,128)} %copy-done.1, f32[1,32,128]{2,1,0:T(8,128)S(1)} %collective-permute-done.5, f32[42,32,1]{2,1,0:T(8,128)} %copy.24, ...), kind=kLoop, calls=%fused_computation.19 | loop fusion | flops 2621440 | bytes 2685441 | tf_op jit(solution)/shard_map/jit(_where)/select_n | solution.py:91
  133.1 0.0 copy-start.3
  133.1 0.8 copy-done.3
  134.0 0.1 fusion.46
  134.1 1.6 %scatter-add.4 = f32[1,40,32,128]{3,2,1,0:T(8,128)} dynamic-update-slice(f32[1,40,32,128]{3,2,1,0:T(8,128)} %bitcast.75, f32[1,40,1,128]{3,2,1,0:T(1,128)S(1)} %fusion.46, s32[]{:T(128)} %constant.63.clone.1, s32[]{:T(128)} %constant.63.clone.1, s32[]{:T(128)} %constant.63.clone.1, s32[]{:T(128)} %constant.63.clone.1) | dynamic-update-slice | bytes 40964 | tf_op jit(solution)/shard_map/scatter-add | solution.py:98
  (24 shorter events, 0.1 us)
Async XLA Ops:
  0.6 56.5 %copy-start = (bf16[1,1280,1280]{2,1,0:T(8,128)(2,1)S(1)}, bf16[1,1280,1280]{2,1,0:T(8,128)(2,1)}, u32[]{:S(2)}) copy-start(bf16[1,1280,1280]{2,1,0:T(8,128)(2,1)} %param.10) | copy-start | bytes 9830404
  0.6 31.5 %copy-start.6 = (s32[1,40,1]{1,2,0:T(1,128)S(1)}, s32[1,40,1]{1,2,0:T(1,128)}, u32[]{:S(2)}) copy-start(s32[1,40,1]{1,2,0:T(1,128)} %param.14) | copy-start | bytes 484
  0.7 29.5 %copy-start.5 = (f32[1,40,128]{2,1,0:T(8,128)S(1)}, f32[1,40,128]{2,1,0:T(8,128)}, u32[]{:S(2)}) copy-start(f32[1,40,128]{2,1,0:T(8,128)} %param.13) | copy-start | bytes 61444
  0.7 31.4 %copy-start.4 = (s32[1,40,128]{2,1,0:T(8,128)S(1)}, s32[1,40,128]{2,1,0:T(8,128)}, u32[]{:S(2)}) copy-start(s32[1,40,128]{2,1,0:T(8,128)} %param.15) | copy-start | bytes 61444
  4.5 0.9 copy-start.2
  5.4 26.8 %collective-permute-start = (f32[1,32,128]{2,1,0:T(8,128)S(1)}, f32[1,32,128]{2,1,0:T(8,128)S(1)}, u32[]{:S(2)}, u32[]{:S(2)}) collective-permute-start(f32[1,32,128]{2,1,0:T(8,128)S(1)} %get-tuple-element.23), channel_id=1, source_target_pairs={{16,0},{32,16},{48,32},{64,48},{80,64},{96,80},{112,96},{128,112},... | collective-permute-start | bytes 49160 | tf_op jit(solution)/shard_map/ppermute | solution.py:17
  21.5 10.8 %collective-permute-start.1 = (f32[1,32,128]{2,1,0:T(8,128)S(1)}, f32[1,32,128]{2,1,0:T(8,128)S(1)}, u32[]{:S(2)}, u32[]{:S(2)}) collective-permute-start(f32[1,32,128]{2,1,0:T(8,128)S(1)} %get-tuple-element.22), channel_id=1, source_target_pairs={{0,16},{16,32},{32,48},{48,64},{64,80},{80,96},{96,112},{112,128},... | collective-permute-start | bytes 49160 | tf_op jit(solution)/shard_map/ppermute | solution.py:14
  25.5 31.7 %all-to-all-start = ((bf16[32,40,128]{2,1,0:T(8,128)(2,1)}), bf16[32,40,128]{2,1,0:T(8,128)(2,1)}, u32[]{:S(2)}, u32[]{:S(2)}) async-start(bf16[32,40,128]{2,1,0:T(8,128)(2,1)} %copy.15), calls=%async_computation | async-start | bytes 655360 | tf_op jit(solution)/shard_map/all_to_all | solution.py:58
  30.2 51.7 %collective-permute-start.8 = (f32[40,128]{1,0:T(8,128)S(1)}, f32[40,128]{1,0:T(8,128)S(1)}, u32[]{:S(2)}, u32[]{:S(2)}) collective-permute-start(f32[40,128]{1,0:T(8,128)S(1)} %bitcast.79), channel_id=1, source_target_pairs={{0,512},{512,0},{1,513},{513,1},{2,514},{514,2},{3,515},{515,3},{4... | collective-permute-start | bytes 61448 | tf_op jit(solution)/shard_map/ppermute | solution.py:29
  36.2 6.8 %collective-permute-start.2 = (f32[42,32,1]{0,1,2:T(8,128)S(1)}, f32[42,32,1]{0,1,2:T(8,128)S(1)}, u32[]{:S(2)}, u32[]{:S(2)}) collective-permute-start(f32[42,32,1]{0,1,2:T(8,128)S(1)} %copy.19), channel_id=1, source_target_pairs={{1,0},{2,1},{3,2},{4,3},{5,4},{6,5},{7,6},{8,7},{9,8},{10,9},{11,1... | collective-permute-start | bytes 16136 | tf_op jit(solution)/shard_map/ppermute | solution.py:17
  39.0 5.5 %collective-permute-start.3 = (f32[42,32,1]{0,1,2:T(8,128)S(1)}, f32[42,32,1]{0,1,2:T(8,128)S(1)}, u32[]{:S(2)}, u32[]{:S(2)}) collective-permute-start(f32[42,32,1]{0,1,2:T(8,128)S(1)} %copy.21), channel_id=1, source_target_pairs={{0,1},{1,2},{2,3},{3,4},{4,5},{5,6},{6,7},{7,8},{8,9},{9,10},{10,1... | collective-permute-start | bytes 16136 | tf_op jit(solution)/shard_map/ppermute | solution.py:14
  50.3 0.9 copy-start.1
  51.1 59.5 %collective-permute-start.4 = (f32[1,32,128]{2,1,0:T(8,128)S(1)}, f32[1,32,128]{2,1,0:T(8,128)S(1)}, u32[]{:S(2)}, u32[]{:S(2)}) collective-permute-start(f32[1,32,128]{2,1,0:T(8,128)S(1)} %get-tuple-element.21), channel_id=1, source_target_pairs={{16,0},{32,16},{48,32},{64,48},{80,64},{96,80},{112,96},{128,112},... | collective-permute-start | bytes 49160 | tf_op jit(solution)/shard_map/ppermute | solution.py:17
  54.0 56.6 %collective-permute-start.5 = (f32[1,32,128]{2,1,0:T(8,128)S(1)}, f32[1,32,128]{2,1,0:T(8,128)S(1)}, u32[]{:S(2)}, u32[]{:S(2)}) collective-permute-start(f32[1,32,128]{2,1,0:T(8,128)S(1)} %get-tuple-element.20), channel_id=1, source_target_pairs={{0,16},{16,32},{32,48},{48,64},{64,80},{80,96},{96,112},{112,128},... | collective-permute-start | bytes 49160 | tf_op jit(solution)/shard_map/ppermute | solution.py:14
  74.1 51.2 %all-to-all-start.1 = ((bf16[32,2,2560]{2,1,0:T(2,128)(2,1)}), bf16[32,2,2560]{2,1,0:T(2,128)(2,1)}, u32[]{:S(2)}, u32[]{:S(2)}) async-start(bf16[32,2,2560]{2,1,0:T(2,128)(2,1)} %reshape.289), calls=%async_computation.1 | async-start | bytes 655360 | tf_op jit(solution)/shard_map/all_to_all | solution.py:65
  114.6 7.7 %collective-permute-start.6 = (f32[42,32,1]{0,1,2:T(8,128)S(1)}, f32[42,32,1]{0,1,2:T(8,128)S(1)}, u32[]{:S(2)}, u32[]{:S(2)}) collective-permute-start(f32[42,32,1]{0,1,2:T(8,128)S(1)} %copy.23), channel_id=1, source_target_pairs={{1,0},{2,1},{3,2},{4,3},{5,4},{6,5},{7,6},{8,7},{9,8},{10,9},{11,1... | collective-permute-start | bytes 16136 | tf_op jit(solution)/shard_map/ppermute | solution.py:17
  117.4 6.4 %collective-permute-start.7 = (f32[42,32,1]{0,1,2:T(8,128)S(1)}, f32[42,32,1]{0,1,2:T(8,128)S(1)}, u32[]{:S(2)}, u32[]{:S(2)}) collective-permute-start(f32[42,32,1]{0,1,2:T(8,128)S(1)} %copy.25), channel_id=1, source_target_pairs={{0,1},{1,2},{2,3},{3,4},{4,5},{5,6},{6,7},{7,8},{8,9},{9,10},{10,1... | collective-permute-start | bytes 16136 | tf_op jit(solution)/shard_map/ppermute | solution.py:14
  133.1 0.8 copy-start.3
where the time goes:
time: 138 us; the launch traced here: 136 us
  local copies, waits for them, and re-layouts  57.3 us (42%)
  starting transfers between devices  49 us (36%)
  other arithmetic  22 us (16%)
  matrix products  6.41 us (5%)
    gather x1, local copies, waits for them, and re-layouts, shards(): jnp.take(partner.reshape(-1), remap_source[0].reshape(-1))  28.7 us
    ppermute x4, starting transfers between devices, padded_2(): lax.ppermute(lax.slice_in_dim(block, 0, width, axis=dim), axis, backward)  21.5 us
    ppermute x4, starting transfers between devices, padded_2(): lax.ppermute(lax.slice_in_dim(block, block.shape[dim] - width, None, axis...  13.2 us
    unnamed x1, other arithmetic  9.14 us
    unnamed x17, local copies, waits for them, and re-layouts  8.11 us
    all_to_all x1, starting transfers between devices, atmosphere(): lax.all_to_all(synthesized, 'row', split_axis=1, concat_axis=0, tiled=True)  7.75 us
    slice x4, local copies, waits for them, and re-layouts, padded_2(): lax.slice_in_dim(block, 0, width, axis=dim)  5.67 us
    all_to_all x1, starting transfers between devices, atmosphere(): lax.all_to_all(weighted, 'row', split_axis=0, concat_axis=1, tiled=True)  4.66 us
  transfers between devices with their start and end apart: 11, of which 0 were waited for; matrix products, arithmetic and copies ran while one was open for 51% of the time, Pallas kernels for 0%

commit v1 on v0

v1 whole, which is shorter than its diff:
```python
import functools

import jax
import jax.numpy as jnp
from jax import lax
from jax.experimental import pallas as pl
from jax.experimental.pallas import tpu as pltpu
from jax.sharding import PartitionSpec as P

MESH = pl.DeviceIdType.MESH
F32 = jnp.float32
BF16 = jnp.bfloat16

ROWS = 32
LAT = 40
WAVES = 32
COLS = 128
NWAVE = 1280
CELLS = LAT * WAVES
CHUNK = 256
CHUNKS = NWAVE // CHUNK
CHUNK_ORDER = (2, 4, 3, 1, 0)
STEP = 0.2


def far_partner(me, step):
    ring, inner = step // 4, step % 4
    size = (8 - ring) // 2
    shift = jnp.where(ring % 2 == 1, size, 8 - size)
    x, y, core = me // 16, (me // 2) % 8, me % 2
    return ((x + 1 - inner // 2) % 2) * 16 + ((y + shift) % 8) * 2 + (core + 1 - inner % 2) % 2


def kernel(
    state, legendre, gauss, mixing, surface, counts, source,
    new_state, new_surface,
    x_v, leg_v, gauss_s, mix_v, surf_v, count_s, source_v, partner_v,
    weight_v, send_v, recv_v, lat_v, acc_v, damp_v, filt_v, back_v, home_v, out_v,
    mask_v, block_v, u_v, edge_v, side_v, gap_v, surf_o,
    in_sem, out_sem, send_sem, recv_sem, back_send_sem, back_recv_sem, pair_sem, halo_send, halo_recv,
):
    comp = lax.axis_index("comp")
    me = lax.axis_index("row")
    col = lax.axis_index("col")
    n_col = lax.axis_size("col")
    air = comp == 0

    barrier = pltpu.get_barrier_semaphore()

    def greet(c, r, k):
        pl.semaphore_signal(barrier, inc=1, device_id=(c, r, k), device_id_type=MESH)

    loads = [
        pltpu.make_async_copy(src, dst, in_sem.at[i])
        for i, (src, dst) in enumerate(
            [(state, x_v), (gauss, gauss_s), (counts, count_s), (surface, surf_v), (source, source_v),
             (legendre, leg_v), (mixing, mix_v)]
        )
    ]
    load_state, load_gauss, load_counts, load_surface, load_source, load_legendre, load_mixing = loads

    greet(1 - comp, me, col)

    @pl.when(air)
    def _():
        def one(s, c):
            greet(0, far_partner(me, s), col)
            return c

        lax.fori_loop(0, ROWS - 1, one, 0)

    has = [me > 0, me < ROWS - 1, col > 0, col < n_col - 1]
    beside = [(1, me - 1, col), (1, me + 1, col), (1, me, col - 1), (1, me, col + 1)]

    @pl.when(jnp.logical_not(air))
    def _():
        for there, place in zip(has, beside):
            @pl.when(there)
            def _():
                greet(*place)

    for load in (load_state, load_gauss, load_counts, load_surface, load_source):
        load.start()

    pair_copy = pltpu.make_async_remote_copy(
        src_ref=surf_v, dst_ref=partner_v, send_sem=pair_sem.at[0], recv_sem=pair_sem.at[1],
        device_id=(1 - comp, me, col), device_id_type=MESH,
    )

    lane = lax.broadcasted_iota(jnp.int32, (1, COLS), 1)

    def surface_step(rate):
        pair_copy.wait_recv()
        for r in range(LAT):
            gap_v[r : r + 1, :] = (lane < count_s[r]).astype(F32)
        where_row = source_v[...] >> 7
        where_lane = source_v[...] & 127

        def one(r, total):
            row = jnp.broadcast_to(partner_v[pl.ds(r, 1), :], (LAT, COLS))
            got = jnp.take_along_axis(row, where_lane, axis=1)
            return jnp.where(where_row == r, got, total)

        pulled = lax.fori_loop(0, LAT, one, jnp.zeros((LAT, COLS), F32))
        gap = gap_v[...] * (pulled - surf_v[...])
        gap_v[...] = gap
        surf_o[...] = surf_v[...] + rate * gap

    @pl.when(air)
    def _():
        load_legendre.start()
        load_gauss.wait()
        for r in range(LAT):
            weight_v[r : r + 1, :] = jnp.full((1, COLS), gauss_s[r], F32)
        load_surface.wait()
        load_state.wait()
        pl.semaphore_wait(barrier, ROWS)
        weights = weight_v[...]

        def out_copy(p):
            return pltpu.make_async_remote_copy(
                src_ref=send_v.at[p], dst_ref=recv_v.at[me], send_sem=send_sem.at[p], recv_sem=recv_sem.at[me],
                device_id=(0, p, col), device_id_type=MESH,
            )

        def arrived(s):
            return pltpu.make_async_remote_copy(
                src_ref=send_v.at[s], dst_ref=recv_v.at[s], send_sem=send_sem.at[s], recv_sem=recv_sem.at[s],
                device_id=(0, me, col), device_id_type=MESH,
            )

        def send_one(s, c):
            p = far_partner(me, s)
            send_v[p] = (x_v[pl.ds(p, LAT, stride=WAVES), :] * weights).astype(BF16)
            out_copy(p).start()
            return c

        lax.fori_loop(0, ROWS - 1, send_one, 0)
        pair_copy.start()
        recv_v[me] = (x_v[pl.ds(me, LAT, stride=WAVES), :] * weights).astype(BF16)

        n = (lax.broadcasted_iota(jnp.int32, (1, NWAVE), 1) + me).astype(F32)
        ratio = n * (n + 1.0) / (1279.0 * 1280.0)
        damp_v[...] = 1.0 / (1.0 + 20.0 * ratio * ratio)
        load_legendre.wait()

        seen = set()
        for place, j in enumerate(CHUNK_ORDER):
            for s in range(CHUNK * j // LAT, (CHUNK * (j + 1) - 1) // LAT + 1):
                if s in seen:
                    continue
                seen.add(s)

                @pl.when(s != me)
                def _():
                    arrived(s).wait_recv()

                lat_v[s * LAT : (s + 1) * LAT, :] = recv_v[s].astype(F32)
            part = lat_v[j * CHUNK : (j + 1) * CHUNK, :].T.astype(BF16)
            product = jnp.dot(part, leg_v[j * CHUNK : (j + 1) * CHUNK, :], preferred_element_type=F32)
            if place == 0:
                acc_v[...] = product
            elif place < CHUNKS - 1:
                acc_v[...] += product
            else:
                filt_v[...] = (damp_v[...] * (acc_v[...] + product)).T.astype(BF16)

        def back_copy(p):
            return pltpu.make_async_remote_copy(
                src_ref=back_v.at[p], dst_ref=home_v.at[me], send_sem=back_send_sem.at[p],
                recv_sem=back_recv_sem.at[me], device_id=(0, p, col), device_id_type=MESH,
            )

        def back_arrived(s):
            return pltpu.make_async_remote_copy(
                src_ref=back_v.at[s], dst_ref=home_v.at[s], send_sem=back_send_sem.at[s],
                recv_sem=back_recv_sem.at[s], device_id=(0, me, col), device_id_type=MESH,
            )

        def synthesize(k, c):
            quarter = (me // 16 + 1 + k) % 2 * 2 + (me // 8 + 1 + k // 2) % 2
            block = jnp.dot(
                leg_v[pl.ds(pl.multiple_of(quarter * (8 * LAT), 8 * LAT), 8 * LAT), :], filt_v[...],
                preferred_element_type=F32,
            )
            for j in range(8):
                p = quarter * 8 + j
                back_v[p] = block[j * LAT : (j + 1) * LAT, :].astype(BF16)

                @pl.when(p != me)
                def _():
                    back_copy(p).start()

            return c

        lax.fori_loop(0, 4, synthesize, 0)
        home_v[me] = back_v[me]

        load_counts.wait()
        load_source.wait()
        surface_step(0.5)
        save = pltpu.make_async_copy(surf_o, new_surface, out_sem.at[4])
        save.start()

        for g in range(4):
            for m in range(g * 8, g * 8 + 8):
                @pl.when(m != me)
                def _():
                    back_arrived(m).wait_recv()

                out_v[pl.ds(m, LAT, stride=WAVES), :] = home_v[m].astype(F32)
        saves = pltpu.make_async_copy(out_v, new_state, out_sem.at[0])
        saves.start()

        def drain(s, c):
            p = far_partner(me, s)
            out_copy(p).wait_send()
            back_copy(p).wait_send()
            return c

        lax.fori_loop(0, ROWS - 1, drain, 0)
        pair_copy.wait_send()
        saves.wait()
        save.wait()

    @pl.when(jnp.logical_not(air))
    def _():
        load_mixing.start()
        load_surface.wait()
        total = sum(there.astype(jnp.int32) for there in has)
        load_counts.wait()
        for r in range(LAT):
            mask_v[r * WAVES : (r + 1) * WAVES, :] = jnp.broadcast_to((lane < count_s[r]).astype(F32), (WAVES, COLS))
        load_mixing.wait()
        pick = (lax.broadcasted_iota(jnp.int32, (CHUNK, WAVES), 0) & (WAVES - 1)) == lax.broadcasted_iota(
            jnp.int32, (CHUNK, WAVES), 1
        )
        pick = pick.astype(F32)
        tall = jnp.dot(pick, mix_v[...], precision=lax.Precision.HIGHEST, preferred_element_type=F32)
        wide = lax.dot_general(
            tall, pick, (((1,), (1,)), ((), ())), precision=lax.Precision.HIGHEST, preferred_element_type=F32
        )
        same = (lax.broadcasted_iota(jnp.int32, (CHUNK, CHUNK), 0) >> 5) == (
            lax.broadcasted_iota(jnp.int32, (CHUNK, CHUNK), 1) >> 5
        )
        block_v[...] = jnp.where(same, wide, 0.0)
        load_state.wait()
        for i in range(CHUNKS):
            part = slice(i * CHUNK, (i + 1) * CHUNK)
            mixed = jnp.dot(block_v[...], x_v[part, :], precision=lax.Precision.HIGHEST, preferred_element_type=F32)
            out_v[part, :] = x_v[part, :] + mask_v[part, :] * mixed
        pl.semaphore_wait(barrier, total + 1)
        pair_copy.start()

        def halo_copy(sweep, side):
            u = u_v.at[sweep]
            if side == 0:
                src, dst = u.at[pl.ds(WAVES, WAVES)], u.at[pl.ds(CELLS + WAVES, WAVES)]
            elif side == 1:
                src, dst = u.at[pl.ds(CELLS, WAVES)], u.at[pl.ds(0, WAVES)]
            else:
                src, dst = edge_v.at[sweep, side - 2], side_v.at[sweep, 3 - side]
            return pltpu.make_async_remote_copy(
                src_ref=src, dst_ref=dst, send_sem=halo_send.at[sweep, side], recv_sem=halo_recv.at[sweep, side ^ 1],
                device_id=beside[side], device_id_type=MESH,
            )

        def halo_arrived(sweep, side):
            u = u_v.at[sweep]
            if side == 0:
                dst = u.at[pl.ds(0, WAVES)]
            elif side == 1:
                dst = u.at[pl.ds(CELLS + WAVES, WAVES)]
            else:
                dst = side_v.at[sweep, side - 2]
            return pltpu.make_async_remote_copy(
                src_ref=dst, dst_ref=dst, send_sem=halo_send.at[sweep, side], recv_sem=halo_recv.at[sweep, side],
                device_id=(1, me, col), device_id_type=MESH,
            )

        for sweep in range(2):
            for i in range(CELLS // COLS):
                part = slice(i * COLS, (i + 1) * COLS)
                u = mask_v[part, :] * out_v[part, :]
                u_v[sweep, WAVES + i * COLS : WAVES + (i + 1) * COLS, :] = u
                flipped = u.T
                edge_v[sweep, 0, i : i + 1, :] = flipped[0:1, :]
                edge_v[sweep, 1, i : i + 1, :] = flipped[COLS - 1 : COLS, :]
            for side in range(4):
                @pl.when(has[side])
                def _():
                    halo_copy(sweep, side).start()

                @pl.when(jnp.logical_not(has[side]))
                def _():
                    if side == 0:
                        u_v[sweep, 0:WAVES, :] = jnp.zeros((WAVES, COLS), F32)
                    elif side == 1:
                        u_v[sweep, CELLS + WAVES : CELLS + 2 * WAVES, :] = jnp.zeros((WAVES, COLS), F32)
                    else:
                        side_v[sweep, side - 2] = jnp.zeros((16, COLS), F32)

            if sweep == 0:
                load_source.wait()
                surface_step(0.25)
                save = pltpu.make_async_copy(surf_o, new_surface, out_sem.at[4])
                save.start()
            for side in range(4):
                @pl.when(has[side])
                def _():
                    halo_arrived(sweep, side).wait_recv()

            west = side_v[sweep, 0].T
            east = side_v[sweep, 1].T
            for i in range(CELLS // COLS):
                part = slice(i * COLS, (i + 1) * COLS)
                low = i * COLS
                centre = u_v[sweep, low + WAVES : low + WAVES + COLS, :]
                left = jnp.where(lane == 0, west[:, i : i + 1], pltpu.roll(centre, 1, 1))
                right = jnp.where(lane == COLS - 1, east[:, i : i + 1], pltpu.roll(centre, COLS - 1, 1))
                above = u_v[sweep, low : low + COLS, :]
                below = u_v[sweep, low + 2 * WAVES : low + 2 * WAVES + COLS, :]
                laplace = above + below + left + right - 4.0 * centre
                out_v[part, :] = out_v[part, :] + STEP * mask_v[part, :] * laplace
        out_v[pl.ds(0, LAT, stride=WAVES), :] = out_v[pl.ds(0, LAT, stride=WAVES), :] + 0.3 * gap_v[...]
        saves = pltpu.make_async_copy(out_v, new_state, out_sem.at[0])
        saves.start()
        for sweep in range(2):
            for side in range(4):
                @pl.when(has[side])
                def _():
                    halo_copy(sweep, side).wait_send()
        load_gauss.wait()
        pair_copy.wait_send()
        saves.wait()
        save.wait()


def shards(model_state, legendre, gauss_weight, mixing, surface, sea_count, remap_source):
    anywhere = pl.BlockSpec(memory_space=pltpu.HBM)
    vmem = pltpu.VMEM
    dma = pltpu.SemaphoreType.DMA
    new_state, new_surface = pl.pallas_call(
        kernel,
        out_shape=(
            jax.ShapeDtypeStruct((CELLS, COLS), F32),
            jax.ShapeDtypeStruct((LAT, COLS), F32),
        ),
        in_specs=[anywhere] * 7,
        out_specs=(anywhere, anywhere),
        scratch_shapes=[
            vmem((CELLS, COLS), F32),
            vmem((NWAVE, NWAVE), BF16),
            pltpu.SMEM((LAT,), F32),
            vmem((WAVES, WAVES), F32),
            vmem((LAT, COLS), F32),
            pltpu.SMEM((LAT,), jnp.int32),
            vmem((LAT, COLS), jnp.int32),
            vmem((LAT, COLS), F32),
            vmem((LAT, COLS), F32),
            vmem((ROWS, LAT, COLS), BF16),
            vmem((ROWS, LAT, COLS), BF16),
            vmem((NWAVE, COLS), F32),
            vmem((COLS, NWAVE), F32),
            vmem((1, NWAVE), F32),
            vmem((NWAVE, COLS), BF16),
            vmem((ROWS, LAT, COLS), BF16),
            vmem((ROWS, LAT, COLS), BF16),
            vmem((CELLS, COLS), F32),
            vmem((CELLS, COLS), F32),
            vmem((CHUNK, CHUNK), F32),
            vmem((2, CELLS + 2 * WAVES, COLS), F32),
            vmem((2, 2, 16, COLS), F32),
            vmem((2, 2, 16, COLS), F32),
            vmem((LAT, COLS), F32),
            vmem((LAT, COLS), F32),
            dma((7,)), dma((5,)), dma((ROWS,)), dma((ROWS,)), dma((ROWS,)), dma((ROWS,)), dma((2,)),
            dma((2, 4)), dma((2, 4)),
        ],
        compiler_params=pltpu.CompilerParams(
            collective_id=0, has_side_effects=True, vmem_limit_bytes=63488 * 1024
        ),
        cost_estimate=pl.CostEstimate(flops=900_000_000, bytes_accessed=5_000_000, transcendentals=0),
    )(
        model_state.reshape(CELLS, COLS),
        legendre.reshape(NWAVE, NWAVE),
        gauss_weight,
        mixing,
        surface.reshape(LAT, COLS),
        sea_count.reshape(LAT),
        remap_source.reshape(LAT, COLS),
    )
    return new_state.reshape(1, LAT, WAVES, COLS), new_surface.reshape(1, LAT, COLS)


def solution(mesh):
    in_specs = (
        P("comp", "row", None, "col"),
        P("row", None, None),
        P("row"),
        P(),
        P("comp", "row", "col"),
        P("comp", "row", "col"),
        P("comp", "row", "col"),
    )
    out_specs = (P("comp", "row", None, "col"), P("comp", "row", "col"))
    return jax.shard_map(shards, mesh=mesh, in_specs=in_specs, out_specs=out_specs, check_vma=False)
```

time: 138 us -> 45 us (0.33); the launches traced: 136 us -> 44.7 us
  local copies, waits for them, and re-layouts: 57.3 us -> 3.3 us
  starting transfers between devices: 49 us -> 0 us
  Pallas kernels: 0 us -> 40.8 us
  other arithmetic: 22 us -> 0 us
  matrix products: 6.41 us -> 0 us
    pallas_call x0 -> x1, Pallas kernels: none -> 40.8 us  [shards(): pl.pallas_call(kernel, out_shape=(jax.ShapeDtypeStruct((CELLS, COLS), F32...]
    ppermute x9 -> x0, starting transfers between devices: 36.6 us -> none  [the longest x4 21.5 us: padded_2(): lax.ppermute(lax.slice_in_dim(block, 0, width, axis=dim), axis, backward)]
    gather x1 -> x0, local copies, waits for them, and re-layouts: 28.7 us -> none  [shards(): jnp.take(partner.reshape(-1), remap_source[0].reshape(-1))]
    all_to_all x2 -> x0, starting transfers between devices: 12.4 us -> none  [the longest x1 7.75 us: atmosphere(): lax.all_to_all(synthesized, 'row', split_axis=1, concat_axis=0, tiled=True)]
    unnamed x1 -> x0, other arithmetic: 9.14 us -> none
    slice x8 -> x0, local copies, waits for them, and re-layouts: 8.75 us -> none  [the longest x4 5.67 us: padded_2(): lax.slice_in_dim(block, 0, width, axis=dim)]
    dot_general x2 -> x0, matrix products: 6.41 us -> none  [the longest x1 3.42 us: atmosphere(): jnp.einsum('wln,wnc->wlc', legendre, filtered, preferred_element_type=jnp...]
    ppermute x4 -> x0, local copies, waits for them, and re-layouts: 6.06 us -> none  [the longest x2 3.04 us: padded_2(): lax.ppermute(lax.slice_in_dim(block, 0, width, axis=dim), axis, backward)]
  transfers between devices with their start and end apart: 11 -> 0, of which waited for: 0 -> 0; matrix products, arithmetic and copies ran while one was open for 51% -> 0% of each run, Pallas kernels for 0% -> 0%
where the time goes in v1:
time: 45 us; the launch traced here: 44.7 us
  Pallas kernels  40.8 us (91%)
  local copies, waits for them, and re-layouts  3.3 us (7%)
  between operations  0.64 us (1%)
    pallas_call x1, Pallas kernels, shards(): pl.pallas_call(kernel, out_shape=(jax.ShapeDtypeStruct((CELLS, COLS), F32...  40.8 us
    unnamed x2, local copies, waits for them, and re-layouts  3.3 us

profile of v1, /device:TPU:1, one launch (start us, length us, event | category | flops | bytes accessed | tf_op | source)
XLA Modules:
  0.0 44.7 jit_solution(10456132369029543439)
XLA Ops:
  0.6 40.8 %shard_map.86 = (f32[1280,128]{1,0:T(8,128)}, f32[40,128]{1,0:T(8,128)}) custom-call(f32[1280,128]{1,0:T(8,128)} %bitcast.8, bf16[1280,1280]{1,0:T(8,128)(2,1)} %bitcast.7, f32[40]{0:T(128)} %gauss.1, f32[32,32]{1,0:T(8,128)} %mixing.1, f32[40,128]{1,0:T(8,128)} %bitcast.11, s32[40]{0:T(128)} %bitcast.13, s32[40,128]{1,0:T(8,128)} %bitcast.12), custom_call_target="tpu_custom_call" | custom-call | flops 900000000 | bytes 5000000 | tf_op jit(solution)/shard_map/pallas_call | solution.py:343
  41.4 2.0 %copy.11 = f32[1,40,32,128]{3,2,1,0:T(8,128)} copy(f32[1,40,32,128]{3,2,1,0:T(8,128)} %bitcast.9) | data formatting | bytes 1310720
  43.4 1.3 %copy.12 = f32[1,40,128]{2,1,0:T(8,128)} copy(f32[1,40,128]{2,1,0:T(8,128)} %bitcast.10) | data formatting | bytes 40960

commit v2 on v1

--- a/solution.py
+++ b/solution.py
@@ -35,9 +35,9 @@
     state, legendre, gauss, mixing, surface, counts, source,
     new_state, new_surface,
     x_v, leg_v, gauss_s, mix_v, surf_v, count_s, source_v, partner_v,
-    weight_v, send_v, recv_v, lat_v, acc_v, damp_v, filt_v, back_v, home_v, out_v,
-    mask_v, block_v, u_v, edge_v, side_v, gap_v, surf_o,
-    in_sem, out_sem, send_sem, recv_sem, back_send_sem, back_recv_sem, pair_sem, halo_send, halo_recv,
+    weight_v, send_v, recv_v, lat_v, acc_v, damp_v, filt_v, back_v, home_v,
+    mask_v, block_v, u_v, edge_v, side_v, gap_v,
+    in_sem, send_sem, recv_sem, back_send_sem, back_recv_sem, pair_sem, halo_send, halo_recv,
 ):
     comp = lax.axis_index("comp")
     me = lax.axis_index("row")
@@ -61,10 +61,18 @@
 
     greet(1 - comp, me, col)
 
-    @pl.when(air)
+    staged = col == 0
+    follows = jnp.logical_and(staged, me > 0)
+
+    @pl.when(jnp.logical_and(air, jnp.logical_not(jnp.logical_and(staged, me == 0))))
     def _():
         def one(s, c):
-            greet(0, far_partner(me, s), col)
+            p = far_partner(me, s)
+
+            @pl.when(jnp.logical_not(jnp.logical_and(staged, p == 0)))
+            def _():
+                greet(0, p, col)
+
             return c
 
         lax.fori_loop(0, ROWS - 1, one, 0)
@@ -104,7 +112,7 @@
         pulled = lax.fori_loop(0, LAT, one, jnp.zeros((LAT, COLS), F32))
         gap = gap_v[...] * (pulled - surf_v[...])
         gap_v[...] = gap
-        surf_o[...] = surf_v[...] + rate * gap
+        new_surface[...] = surf_v[...] + rate * gap
 
     @pl.when(air)
     def _():
@@ -114,7 +122,20 @@
             weight_v[r : r + 1, :] = jnp.full((1, COLS), gauss_s[r], F32)
         load_surface.wait()
         load_state.wait()
-        pl.semaphore_wait(barrier, ROWS)
+        pl.semaphore_wait(barrier, jnp.where(follows, ROWS - 1, ROWS))
+
+        @pl.when(follows)
+        def _():
+            greet(0, 0, col)
+
+        @pl.when(jnp.logical_and(staged, me == 0))
+        def _():
+            def one(s, c):
+                greet(0, far_partner(me, s), col)
+                return c
+
+            lax.fori_loop(0, ROWS - 1, one, 0)
+
         weights = weight_v[...]
 
         def out_copy(p):
@@ -132,7 +153,11 @@
         def send_one(s, c):
             p = far_partner(me, s)
             send_v[p] = (x_v[pl.ds(p, LAT, stride=WAVES), :] * weights).astype(BF16)
-            out_copy(p).start()
+
+            @pl.when(jnp.logical_not(jnp.logical_and(follows, p == 0)))
+            def _():
+                out_copy(p).start()
+
             return c
 
         lax.fori_loop(0, ROWS - 1, send_one, 0)
@@ -146,6 +171,13 @@
 
         seen = set()
         for place, j in enumerate(CHUNK_ORDER):
+            if place == CHUNKS - 1:
+
+                @pl.when(follows)
+                def _():
+                    pl.semaphore_wait(barrier, 1)
+                    out_copy(0).start()
+
             for s in range(CHUNK * j // LAT, (CHUNK * (j + 1) - 1) // LAT + 1):
                 if s in seen:
                     continue
@@ -199,18 +231,25 @@
         load_counts.wait()
         load_source.wait()
         surface_step(0.5)
-        save = pltpu.make_async_copy(surf_o, new_surface, out_sem.at[4])
-        save.start()
-
-        for g in range(4):
-            for m in range(g * 8, g * 8 + 8):
-                @pl.when(m != me)
-                def _():
-                    back_arrived(m).wait_recv()
-
-                out_v[pl.ds(m, LAT, stride=WAVES), :] = home_v[m].astype(F32)
-        saves = pltpu.make_async_copy(out_v, new_state, out_sem.at[0])
-        saves.start()
+
+        def take_home(m):
+            @pl.when(m != me)
+            def _():
+                back_arrived(m).wait_recv()
+
+            new_state[pl.ds(m, LAT, stride=WAVES), :] = home_v[m].astype(F32)
+
+        def near(s, c):
+            m = far_partner(me, ROWS - 1 - s)
+
+            @pl.when(m != 0)
+            def _():
+                take_home(m)
+
+            return c
+
+        lax.fori_loop(0, ROWS, near, 0)
+        take_home(0)
 
         def drain(s, c):
             p = far_partner(me, s)
@@ -220,8 +259,6 @@
 
         lax.fori_loop(0, ROWS - 1, drain, 0)
         pair_copy.wait_send()
-        saves.wait()
-        save.wait()
 
     @pl.when(jnp.logical_not(air))
     def _():
@@ -248,7 +285,7 @@
         for i in range(CHUNKS):
             part = slice(i * CHUNK, (i + 1) * CHUNK)
             mixed = jnp.dot(block_v[...], x_v[part, :], precision=lax.Precision.HIGHEST, preferred_element_type=F32)
-            out_v[part, :] = x_v[part, :] + mask_v[part, :] * mixed
+            new_state[part, :] = x_v[part, :] + mask_v[part, :] * mixed
         pl.semaphore_wait(barrier, total + 1)
         pair_copy.start()
 
@@ -281,7 +318,7 @@
         for sweep in range(2):
             for i in range(CELLS // COLS):
                 part = slice(i * COLS, (i + 1) * COLS)
-                u = mask_v[part, :] * out_v[part, :]
+                u = mask_v[part, :] * new_state[part, :]
                 u_v[sweep, WAVES + i * COLS : WAVES + (i + 1) * COLS, :] = u
                 flipped = u.T
                 edge_v[sweep, 0, i : i + 1, :] = flipped[0:1, :]
@@ -303,8 +340,6 @@
             if sweep == 0:
                 load_source.wait()
                 surface_step(0.25)
-                save = pltpu.make_async_copy(surf_o, new_surface, out_sem.at[4])
-                save.start()
             for side in range(4):
                 @pl.when(has[side])
                 def _():
@@ -321,10 +356,8 @@
                 above = u_v[sweep, low : low + COLS, :]
                 below = u_v[sweep, low + 2 * WAVES : low + 2 * WAVES + COLS, :]
                 laplace = above + below + left + right - 4.0 * centre
-                out_v[part, :] = out_v[part, :] + STEP * mask_v[part, :] * laplace
-        out_v[pl.ds(0, LAT, stride=WAVES), :] = out_v[pl.ds(0, LAT, stride=WAVES), :] + 0.3 * gap_v[...]
-        saves = pltpu.make_async_copy(out_v, new_state, out_sem.at[0])
-        saves.start()
+                new_state[part, :] = new_state[part, :] + STEP * mask_v[part, :] * laplace
+        new_state[pl.ds(0, LAT, stride=WAVES), :] = new_state[pl.ds(0, LAT, stride=WAVES), :] + 0.3 * gap_v[...]
         for sweep in range(2):
             for side in range(4):
                 @pl.when(has[side])
@@ -332,22 +365,20 @@
                     halo_copy(sweep, side).wait_send()
         load_gauss.wait()
         pair_copy.wait_send()
-        saves.wait()
-        save.wait()
 
 
 def shards(model_state, legendre, gauss_weight, mixing, surface, sea_count, remap_source):
-    anywhere = pl.BlockSpec(memory_space=pltpu.HBM)
+    anywhere = pl.BlockSpec(memory_space=pl.ANY)
     vmem = pltpu.VMEM
     dma = pltpu.SemaphoreType.DMA
     new_state, new_surface = pl.pallas_call(
         kernel,
         out_shape=(
-            jax.ShapeDtypeStruct((CELLS, COLS), F32),
-            jax.ShapeDtypeStruct((LAT, COLS), F32),
+            pltpu.VMEM((CELLS, COLS), F32),
+            pltpu.VMEM((LAT, COLS), F32),
         ),
         in_specs=[anywhere] * 7,
-        out_specs=(anywhere, anywhere),
+        out_specs=(pl.BlockSpec(memory_space=vmem),) * 2,
         scratch_shapes=[
             vmem((CELLS, COLS), F32),
             vmem((NWAVE, NWAVE), BF16),
@@ -367,28 +398,31 @@
             vmem((ROWS, LAT, COLS), BF16),
             vmem((ROWS, LAT, COLS), BF16),
             vmem((CELLS, COLS), F32),
-            vmem((CELLS, COLS), F32),
             vmem((CHUNK, CHUNK), F32),
             vmem((2, CELLS + 2 * WAVES, COLS), F32),
             vmem((2, 2, 16, COLS), F32),
             vmem((2, 2, 16, COLS), F32),
             vmem((LAT, COLS), F32),
-            vmem((LAT, COLS), F32),
-            dma((7,)), dma((5,)), dma((ROWS,)), dma((ROWS,)), dma((ROWS,)), dma((ROWS,)), dma((2,)),
+            dma((7,)), dma((ROWS,)), dma((ROWS,)), dma((ROWS,)), dma((ROWS,)), dma((2,)),
             dma((2, 4)), dma((2, 4)),
         ],
         compiler_params=pltpu.CompilerParams(
-            collective_id=0, has_side_effects=True, vmem_limit_bytes=63488 * 1024
+            collective_id=0, has_side_effects=True, vmem_limit_bytes=48 * 1024 * 1024
         ),
         cost_estimate=pl.CostEstimate(flops=900_000_000, bytes_accessed=5_000_000, transcendentals=0),
     )(
-        model_state.reshape(CELLS, COLS),
-        legendre.reshape(NWAVE, NWAVE),
-        gauss_weight,
-        mixing,
-        surface.reshape(LAT, COLS),
-        sea_count.reshape(LAT),
-        remap_source.reshape(LAT, COLS),
+        *(
+            pltpu.with_memory_space_constraint(operand, pltpu.HBM)
+            for operand in (
+                model_state.reshape(CELLS, COLS),
+                legendre.reshape(NWAVE, NWAVE),
+                gauss_weight,
+                mixing,
+                surface.reshape(LAT, COLS),
+                sea_count.reshape(LAT),
+                remap_source.reshape(LAT, COLS),
+            )
+        )
     )
     return new_state.reshape(1, LAT, WAVES, COLS), new_surface.reshape(1, LAT, COLS)
 

time: 45 us -> 37.4 us (0.83)
  Pallas kernels: 40.8 us -> 35.2 us
  local copies, waits for them, and re-layouts: 3.3 us -> 1.44 us
    pallas_call x1, Pallas kernels: 40.8 us -> 35.2 us  [shards(): pl.pallas_call(kernel, out_shape=(pltpu.VMEM((CELLS, COLS), F32), pltpu.V...]
    unnamed x2, local copies, waits for them, and re-layouts: 3.3 us -> 1.44 us
where the time goes in v2:
time: 37.4 us; the launch traced here: 37.2 us
  Pallas kernels  35.2 us (94%)
  local copies, waits for them, and re-layouts  1.44 us (4%)
  between operations  0.64 us (2%)
    pallas_call x1, Pallas kernels, shards(): pl.pallas_call(kernel, out_shape=(pltpu.VMEM((CELLS, COLS), F32), pltpu.V...  35.2 us
    unnamed x2, local copies, waits for them, and re-layouts  1.44 us

profile of v2, /device:TPU:1, one launch (start us, length us, event | category | flops | bytes accessed | tf_op | source)
XLA Modules:
  0.0 37.2 jit_solution(15586985150905206129)
XLA Ops:
  0.6 35.2 %shard_map.86 = (f32[1280,128]{1,0:T(8,128)S(1)}, f32[40,128]{1,0:T(8,128)S(1)}) custom-call(f32[1280,128]{1,0:T(8,128)} %bitcast.10, bf16[1280,1280]{1,0:T(8,128)(2,1)} %bitcast.9, f32[40]{0:T(128)} %gauss.1, f32[32,32]{1,0:T(8,128)} %mixing.1, f32[40,128]{1,0:T(8,128)} %bitcast.11, s32[40]{0:T(128)} %bitcast.13, s32[40,128]{1,0:T(8,128)} %bitcast.12), custom_call_target="tpu_custom_call" | custom-call | flops 900000000 | bytes 5000000 | tf_op jit(solution)/shard_map/pallas_call | solution.py:374
  35.8 0.8 %copy.11 = f32[1,40,32,128]{3,2,1,0:T(8,128)} copy(f32[1,40,32,128]{3,2,1,0:T(8,128)S(1)} %bitcast.7) | data formatting | bytes 1310720
  36.6 0.6 %copy.12 = f32[1,40,128]{2,1,0:T(8,128)} copy(f32[1,40,128]{2,1,0:T(8,128)S(1)} %bitcast.8) | data formatting | bytes 40960

commit v3 on v2

--- a/solution.py
+++ b/solution.py
@@ -25,10 +25,9 @@
 
 def far_partner(me, step):
     ring, inner = step // 4, step % 4
-    size = (8 - ring) // 2
-    shift = jnp.where(ring % 2 == 1, size, 8 - size)
-    x, y, core = me // 16, (me // 2) % 8, me % 2
-    return ((x + 1 - inner // 2) % 2) * 16 + ((y + shift) % 8) * 2 + (core + 1 - inner % 2) % 2
+    shift = (8 - ring) // 2 if ring % 2 else 8 - (8 - ring) // 2
+    flip = (1 - inner // 2) * 16 + (1 - inner % 2)
+    return ((me & 17) ^ flip) + ((me + 2 * shift) & 14)
 
 
 def kernel(
@@ -59,23 +58,24 @@
     ]
     load_state, load_gauss, load_counts, load_surface, load_source, load_legendre, load_mixing = loads
 
-    greet(1 - comp, me, col)
-
     staged = col == 0
-    follows = jnp.logical_and(staged, me > 0)
-
-    @pl.when(jnp.logical_and(air, jnp.logical_not(jnp.logical_and(staged, me == 0))))
-    def _():
-        def one(s, c):
+    late = jnp.logical_and(jnp.logical_and(staged, me == 0), air)
+    helper = jnp.logical_and(jnp.logical_and(staged, me == 0), jnp.logical_not(air))
+    early = jnp.logical_or(jnp.logical_and(jnp.logical_and(staged, me > 0), air), helper)
+    works = jnp.logical_or(jnp.logical_and(air, jnp.logical_not(late)), helper)
+
+    def wave_comp(p):
+        return jnp.where(jnp.logical_and(staged, p == 0), 1, 0)
+
+    @pl.when(jnp.logical_not(jnp.logical_or(late, helper)))
+    def _():
+        greet(1 - comp, me, col)
+
+    @pl.when(works)
+    def _():
+        for s in range(ROWS - 1):
             p = far_partner(me, s)
-
-            @pl.when(jnp.logical_not(jnp.logical_and(staged, p == 0)))
-            def _():
-                greet(0, p, col)
-
-            return c
-
-        lax.fori_loop(0, ROWS - 1, one, 0)
+            greet(wave_comp(p), p, col)
 
     has = [me > 0, me < ROWS - 1, col > 0, col < n_col - 1]
     beside = [(1, me - 1, col), (1, me + 1, col), (1, me, col - 1), (1, me, col + 1)]
@@ -89,6 +89,10 @@
 
     for load in (load_state, load_gauss, load_counts, load_surface, load_source):
         load.start()
+
+    @pl.when(works)
+    def _():
+        load_legendre.start()
 
     pair_copy = pltpu.make_async_remote_copy(
         src_ref=surf_v, dst_ref=partner_v, send_sem=pair_sem.at[0], recv_sem=pair_sem.at[1],
@@ -114,151 +118,73 @@
         gap_v[...] = gap
         new_surface[...] = surf_v[...] + rate * gap
 
+    def out_copy(p):
+        return pltpu.make_async_remote_copy(
+            src_ref=send_v.at[p], dst_ref=recv_v.at[me], send_sem=send_sem.at[p], recv_sem=recv_sem.at[me],
+            device_id=(wave_comp(p), p, col), device_id_type=MESH,
+        )
+
+    def arrived(s):
+        return pltpu.make_async_remote_copy(
+            src_ref=send_v.at[s], dst_ref=recv_v.at[s], send_sem=send_sem.at[s], recv_sem=recv_sem.at[s],
+            device_id=(0, s, col), device_id_type=MESH,
+        )
+
+    def back_copy(p):
+        return pltpu.make_async_remote_copy(
+            src_ref=back_v.at[p], dst_ref=home_v.at[me], send_sem=back_send_sem.at[p],
+            recv_sem=back_recv_sem.at[me], device_id=(0, p, col), device_id_type=MESH,
+        )
+
+    def back_arrived(s):
+        return pltpu.make_async_remote_copy(
+            src_ref=back_v.at[s], dst_ref=home_v.at[s], send_sem=back_send_sem.at[s],
+            recv_sem=back_recv_sem.at[s], device_id=(0, s, col), device_id_type=MESH,
+        )
+
+    def take_home(m):
+        back_arrived(m).wait_recv()
+        new_state[pl.ds(m, LAT, stride=WAVES), :] = home_v[m].astype(F32)
+
+    def elsewhere(r):
+        return jnp.logical_not(jnp.logical_and(works, jnp.logical_and(air, r == me)))
+
     @pl.when(air)
     def _():
-        load_legendre.start()
         load_gauss.wait()
         for r in range(LAT):
             weight_v[r : r + 1, :] = jnp.full((1, COLS), gauss_s[r], F32)
         load_surface.wait()
         load_state.wait()
-        pl.semaphore_wait(barrier, jnp.where(follows, ROWS - 1, ROWS))
-
-        @pl.when(follows)
+        pl.semaphore_wait(barrier, ROWS)
+
+        @pl.when(early)
         def _():
             greet(0, 0, col)
 
-        @pl.when(jnp.logical_and(staged, me == 0))
-        def _():
-            def one(s, c):
-                greet(0, far_partner(me, s), col)
-                return c
-
-            lax.fori_loop(0, ROWS - 1, one, 0)
-
         weights = weight_v[...]
 
-        def out_copy(p):
-            return pltpu.make_async_remote_copy(
-                src_ref=send_v.at[p], dst_ref=recv_v.at[me], send_sem=send_sem.at[p], recv_sem=recv_sem.at[me],
-                device_id=(0, p, col), device_id_type=MESH,
-            )
-
-        def arrived(s):
-            return pltpu.make_async_remote_copy(
-                src_ref=send_v.at[s], dst_ref=recv_v.at[s], send_sem=send_sem.at[s], recv_sem=recv_sem.at[s],
-                device_id=(0, me, col), device_id_type=MESH,
-            )
-
-        def send_one(s, c):
+        for s in range(ROWS - 1):
             p = far_partner(me, s)
             send_v[p] = (x_v[pl.ds(p, LAT, stride=WAVES), :] * weights).astype(BF16)
-
-            @pl.when(jnp.logical_not(jnp.logical_and(follows, p == 0)))
-            def _():
-                out_copy(p).start()
-
-            return c
-
-        lax.fori_loop(0, ROWS - 1, send_one, 0)
+            out_copy(p).start()
+
+        own = (x_v[pl.ds(me, LAT, stride=WAVES), :] * weights).astype(BF16)
+
+        @pl.when(late)
+        def _():
+            send_v[me] = own
+            out_copy(me).start()
+            greet(1, me, col)
+
+            for s in range(ROWS - 1):
+                greet(0, far_partner(me, s), col)
+
+        @pl.when(jnp.logical_not(late))
+        def _():
+            recv_v[me] = own
+
         pair_copy.start()
-        recv_v[me] = (x_v[pl.ds(me, LAT, stride=WAVES), :] * weights).astype(BF16)
-
-        n = (lax.broadcasted_iota(jnp.int32, (1, NWAVE), 1) + me).astype(F32)
-        ratio = n * (n + 1.0) / (1279.0 * 1280.0)
-        damp_v[...] = 1.0 / (1.0 + 20.0 * ratio * ratio)
-        load_legendre.wait()
-
-        seen = set()
-        for place, j in enumerate(CHUNK_ORDER):
-            if place == CHUNKS - 1:
-
-                @pl.when(follows)
-                def _():
-                    pl.semaphore_wait(barrier, 1)
-                    out_copy(0).start()
-
-            for s in range(CHUNK * j // LAT, (CHUNK * (j + 1) - 1) // LAT + 1):
-                if s in seen:
-                    continue
-                seen.add(s)
-
-                @pl.when(s != me)
-                def _():
-                    arrived(s).wait_recv()
-
-                lat_v[s * LAT : (s + 1) * LAT, :] = recv_v[s].astype(F32)
-            part = lat_v[j * CHUNK : (j + 1) * CHUNK, :].T.astype(BF16)
-            product = jnp.dot(part, leg_v[j * CHUNK : (j + 1) * CHUNK, :], preferred_element_type=F32)
-            if place == 0:
-                acc_v[...] = product
-            elif place < CHUNKS - 1:
-                acc_v[...] += product
-            else:
-                filt_v[...] = (damp_v[...] * (acc_v[...] + product)).T.astype(BF16)
-
-        def back_copy(p):
-            return pltpu.make_async_remote_copy(
-                src_ref=back_v.at[p], dst_ref=home_v.at[me], send_sem=back_send_sem.at[p],
-                recv_sem=back_recv_sem.at[me], device_id=(0, p, col), device_id_type=MESH,
-            )
-
-        def back_arrived(s):
-            return pltpu.make_async_remote_copy(
-                src_ref=back_v.at[s], dst_ref=home_v.at[s], send_sem=back_send_sem.at[s],
-                recv_sem=back_recv_sem.at[s], device_id=(0, me, col), device_id_type=MESH,
-            )
-
-        def synthesize(k, c):
-            quarter = (me // 16 + 1 + k) % 2 * 2 + (me // 8 + 1 + k // 2) % 2
-            block = jnp.dot(
-                leg_v[pl.ds(pl.multiple_of(quarter * (8 * LAT), 8 * LAT), 8 * LAT), :], filt_v[...],
-                preferred_element_type=F32,
-            )
-            for j in range(8):
-                p = quarter * 8 + j
-                back_v[p] = block[j * LAT : (j + 1) * LAT, :].astype(BF16)
-
-                @pl.when(p != me)
-                def _():
-                    back_copy(p).start()
-
-            return c
-
-        lax.fori_loop(0, 4, synthesize, 0)
-        home_v[me] = back_v[me]
-
-        load_counts.wait()
-        load_source.wait()
-        surface_step(0.5)
-
-        def take_home(m):
-            @pl.when(m != me)
-            def _():
-                back_arrived(m).wait_recv()
-
-            new_state[pl.ds(m, LAT, stride=WAVES), :] = home_v[m].astype(F32)
-
-        def near(s, c):
-            m = far_partner(me, ROWS - 1 - s)
-
-            @pl.when(m != 0)
-            def _():
-                take_home(m)
-
-            return c
-
-        lax.fori_loop(0, ROWS, near, 0)
-        take_home(0)
-
-        def drain(s, c):
-            p = far_partner(me, s)
-            out_copy(p).wait_send()
-            back_copy(p).wait_send()
-            return c
-
-        lax.fori_loop(0, ROWS - 1, drain, 0)
-        pair_copy.wait_send()
 
     @pl.when(jnp.logical_not(air))
     def _():
@@ -286,8 +212,15 @@
             part = slice(i * CHUNK, (i + 1) * CHUNK)
             mixed = jnp.dot(block_v[...], x_v[part, :], precision=lax.Precision.HIGHEST, preferred_element_type=F32)
             new_state[part, :] = x_v[part, :] + mask_v[part, :] * mixed
-        pl.semaphore_wait(barrier, total + 1)
-        pair_copy.start()
+        pl.semaphore_wait(barrier, total + jnp.where(helper, ROWS - 1, 1))
+
+        @pl.when(helper)
+        def _():
+            greet(0, 0, col)
+
+        @pl.when(jnp.logical_not(helper))
+        def _():
+            pair_copy.start()
 
         def halo_copy(sweep, side):
             u = u_v.at[sweep]
@@ -337,9 +270,6 @@
                     else:
                         side_v[sweep, side - 2] = jnp.zeros((16, COLS), F32)
 
-            if sweep == 0:
-                load_source.wait()
-                surface_step(0.25)
             for side in range(4):
                 @pl.when(has[side])
                 def _():
@@ -357,12 +287,112 @@
                 below = u_v[sweep, low + 2 * WAVES : low + 2 * WAVES + COLS, :]
                 laplace = above + below + left + right - 4.0 * centre
                 new_state[part, :] = new_state[part, :] + STEP * mask_v[part, :] * laplace
-        new_state[pl.ds(0, LAT, stride=WAVES), :] = new_state[pl.ds(0, LAT, stride=WAVES), :] + 0.3 * gap_v[...]
         for sweep in range(2):
             for side in range(4):
                 @pl.when(has[side])
                 def _():
                     halo_copy(sweep, side).wait_send()
+
+    @pl.when(works)
+    def _():
+        n = (lax.broadcasted_iota(jnp.int32, (1, NWAVE), 1) + me).astype(F32)
+        ratio = n * (n + 1.0) / (1279.0 * 1280.0)
+        damp_v[...] = 1.0 / (1.0 + 20.0 * ratio * ratio)
+        load_legendre.wait()
+
+        seen = set()
+        for place, j in enumerate(CHUNK_ORDER):
+            if place == CHUNKS - 1:
+
+                @pl.when(early)
+                def _():
+                    pl.semaphore_wait(barrier, 1)
+
+                @pl.when(helper)
+                def _():
+                    pair_copy.start()
+
+            for s in range(CHUNK * j // LAT, (CHUNK * (j + 1) - 1) // LAT + 1):
+                if s in seen:
+                    continue
+                seen.add(s)
+
+                @pl.when(elsewhere(s))
+                def _():
+                    arrived(s).wait_recv()
+
+                lat_v[s * LAT : (s + 1) * LAT, :] = recv_v[s].astype(F32)
+            part = lat_v[j * CHUNK : (j + 1) * CHUNK, :].T.astype(BF16)
+            product = jnp.dot(part, leg_v[j * CHUNK : (j + 1) * CHUNK, :], preferred_element_type=F32)
+            if place == 0:
+                acc_v[...] = product
+            elif place < CHUNKS - 1:
+                acc_v[...] += product
+            else:
+                filt_v[...] = (damp_v[...] * (acc_v[...] + product)).T.astype(BF16)
+
+        for k in range(4):
+            quarter = (me >> 3) ^ (3, 2, 1, 0)[k]
+            block = jnp.dot(
+                leg_v[pl.ds(pl.multiple_of(quarter * (8 * LAT), 8 * LAT), 8 * LAT), :], filt_v[...],
+                preferred_element_type=F32,
+            )
+            for j in range(8):
+                p = quarter * 8 + j
+                back_v[p] = block[j * LAT : (j + 1) * LAT, :].astype(BF16)
+                if k < 3:
+                    back_copy(p).start()
+                else:
+
+                    @pl.when(elsewhere(p))
+                    def _():
+                        back_copy(p).start()
+
+        @pl.when(air)
+        def _():
+            home_v[me] = back_v[me]
+
+    @pl.when(air)
+    def _():
+        load_counts.wait()
+        load_source.wait()
+        surface_step(0.5)
+
+        for s in range(ROWS - 1):
+            out_copy(far_partner(me, s)).wait_send()
+
+        @pl.when(late)
+        def _():
+            out_copy(me).wait_send()
+            take_home(me)
+
+        @pl.when(jnp.logical_not(late))
+        def _():
+            new_state[pl.ds(me, LAT, stride=WAVES), :] = home_v[me].astype(F32)
+
+        pair_copy.wait_send()
+        for s in range(ROWS - 2, 8, -1):
+            take_home(far_partner(me, s))
+
+    @pl.when(works)
+    def _():
+        for s in range(ROWS - 1):
+            back_copy(far_partner(me, s)).wait_send()
+
+        @pl.when(helper)
+        def _():
+            back_copy(me).wait_send()
+
+    @pl.when(air)
+    def _():
+        for s in range(8, -1, -1):
+            take_home(far_partner(me, s))
+
+    @pl.when(jnp.logical_not(air))
+    def _():
+        load_source.wait()
+        surface_step(0.25)
+        new_state[pl.ds(0, LAT, stride=WAVES), :] = new_state[pl.ds(0, LAT, stride=WAVES), :] + 0.3 * gap_v[...]
         load_gauss.wait()
         pair_copy.wait_send()
 

time: 37.4 us -> 33.5 us (0.90)
  Pallas kernels: 35.2 us -> 31.3 us
    pallas_call x1, Pallas kernels: 35.2 us -> 31.3 us  [shards(): pl.pallas_call(kernel, out_shape=(pltpu.VMEM((CELLS, COLS), F32), pltpu.V...]
where the time goes in v3:
time: 33.5 us; the launch traced here: 33.4 us
  Pallas kernels  31.3 us (93%)
  local copies, waits for them, and re-layouts  1.44 us (4%)
  between operations  0.64 us (2%)
    pallas_call x1, Pallas kernels, shards(): pl.pallas_call(kernel, out_shape=(pltpu.VMEM((CELLS, COLS), F32), pltpu.V...  31.3 us
    unnamed x2, local copies, waits for them, and re-layouts  1.44 us

profile of v3, /device:TPU:1, one launch (start us, length us, event | category | flops | bytes accessed | tf_op | source)
XLA Modules:
  0.0 33.4 jit_solution(13809967378569511486)
XLA Ops:
  0.6 31.3 %shard_map.86 = (f32[1280,128]{1,0:T(8,128)S(1)}, f32[40,128]{1,0:T(8,128)S(1)}) custom-call(f32[1280,128]{1,0:T(8,128)} %bitcast.10, bf16[1280,1280]{1,0:T(8,128)(2,1)} %bitcast.9, f32[40]{0:T(128)} %gauss.1, f32[32,32]{1,0:T(8,128)} %mixing.1, f32[40,128]{1,0:T(8,128)} %bitcast.11, s32[40]{0:T(128)} %bitcast.13, s32[40,128]{1,0:T(8,128)} %bitcast.12), custom_call_target="tpu_custom_call" | custom-call | flops 900000000 | bytes 5000000 | tf_op jit(solution)/shard_map/pallas_call | solution.py:404
  31.9 0.8 %copy.11 = f32[1,40,32,128]{3,2,1,0:T(8,128)} copy(f32[1,40,32,128]{3,2,1,0:T(8,128)S(1)} %bitcast.7) | data formatting | bytes 1310720
  32.8 0.6 %copy.12 = f32[1,40,128]{2,1,0:T(8,128)} copy(f32[1,40,128]{2,1,0:T(8,128)S(1)} %bitcast.8) | data formatting | bytes 40960

commit v4 on v3

--- a/solution.py
+++ b/solution.py
@@ -21,6 +21,7 @@
 CHUNKS = NWAVE // CHUNK
 CHUNK_ORDER = (2, 4, 3, 1, 0)
 STEP = 0.2
+SAVES = 4
 
 
 def far_partner(me, step):
@@ -395,6 +396,21 @@
         new_state[pl.ds(0, LAT, stride=WAVES), :] = new_state[pl.ds(0, LAT, stride=WAVES), :] + 0.3 * gap_v[...]
         load_gauss.wait()
         pair_copy.wait_send()
+
+
+def save(state, surface, new_state, new_surface, sem):
+    part = CELLS // SAVES
+    copies = [
+        pltpu.make_async_copy(
+            state.at[pl.ds(i * part, part)], new_state.at[pl.ds(i * part, part)], sem.at[i]
+        )
+        for i in range(SAVES)
+    ]
+    copies.append(pltpu.make_async_copy(surface, new_surface, sem.at[SAVES]))
+    for copy in copies:
+        copy.start()
+    for copy in copies:
+        copy.wait()
 
 
 def shards(model_state, legendre, gauss_weight, mixing, surface, sea_count, remap_source):
@@ -454,6 +470,19 @@
             )
         )
     )
+    new_state, new_surface = pl.pallas_call(
+        save,
+        out_shape=(
+            pltpu.HBM((CELLS, COLS), F32),
+            pltpu.HBM((LAT, COLS), F32),
+        ),
+        in_specs=[anywhere] * 2,
+        out_specs=(anywhere,) * 2,
+        scratch_shapes=[dma((SAVES + 1,))],
+    )(
+        pltpu.with_memory_space_constraint(new_state, pltpu.VMEM),
+        pltpu.with_memory_space_constraint(new_surface, pltpu.VMEM),
+    )
     return new_state.reshape(1, LAT, WAVES, COLS), new_surface.reshape(1, LAT, COLS)
 
 

time: 33.5 us -> 33 us (0.985)
  local copies, waits for them, and re-layouts: 1.44 us -> 0 us
  Pallas kernels: 31.3 us -> 32.2 us
    unnamed x2 -> x0, local copies, waits for them, and re-layouts: 1.44 us -> none
    pallas_call x0 -> x1, Pallas kernels: none -> 0.88 us  [shards(): pl.pallas_call(save, out_shape=(pltpu.HBM((CELLS, COLS), F32), pltpu.HBM(...]
where the time goes in v4:
time: 33 us; the launch traced here: 32.8 us
  Pallas kernels  32.2 us (98%)
  between operations  0.64 us (2%)
    pallas_call x1, Pallas kernels, shards(): pl.pallas_call(kernel, out_shape=(pltpu.VMEM((CELLS, COLS), F32), pltpu.V...  31.3 us
    pallas_call x1, Pallas kernels, shards(): pl.pallas_call(save, out_shape=(pltpu.HBM((CELLS, COLS), F32), pltpu.HBM(...  0.88 us

profile of v4, /device:TPU:1, one launch (start us, length us, event | category | flops | bytes accessed | tf_op | source)
XLA Modules:
  0.0 32.8 jit_solution(10594352481720854038)
XLA Ops:
  0.6 31.3 %shard_map.86 = (f32[1280,128]{1,0:T(8,128)S(1)}, f32[40,128]{1,0:T(8,128)S(1)}) custom-call(f32[1280,128]{1,0:T(8,128)} %bitcast.8, bf16[1280,1280]{1,0:T(8,128)(2,1)} %bitcast.7, f32[40]{0:T(128)} %gauss.1, f32[32,32]{1,0:T(8,128)} %mixing.1, f32[40,128]{1,0:T(8,128)} %bitcast.9, s32[40]{0:T(128)} %bitcast.11, s32[40,128]{1,0:T(8,128)} %bitcast.10), custom_call_target="tpu_custom_call" | custom-call | flops 900000000 | bytes 5000000 | tf_op jit(solution)/shard_map/pallas_call | solution.py:420
  31.9 0.9 %shard_map.87 = (f32[1280,128]{1,0:T(8,128)}, f32[40,128]{1,0:T(8,128)}) custom-call(f32[1280,128]{1,0:T(8,128)S(1)} %get-tuple-element.6.state, f32[40,128]{1,0:T(8,128)S(1)} %get-tuple-element.7.surface), custom_call_target="tpu_custom_call" | custom-call | tf_op jit(solution)/shard_map/pallas_call | solution.py:473

commit v5 on v4

--- a/solution.py
+++ b/solution.py
@@ -59,6 +59,9 @@
     ]
     load_state, load_gauss, load_counts, load_surface, load_source, load_legendre, load_mixing = loads
 
+    for load in (load_gauss, load_state, load_surface, load_counts, load_source):
+        load.start()
+
     staged = col == 0
     late = jnp.logical_and(jnp.logical_and(staged, me == 0), air)
     helper = jnp.logical_and(jnp.logical_and(staged, me == 0), jnp.logical_not(air))
@@ -88,12 +91,16 @@
             def _():
                 greet(*place)
 
-    for load in (load_state, load_gauss, load_counts, load_surface, load_source):
-        load.start()
-
     @pl.when(works)
     def _():
         load_legendre.start()
+
+    @pl.when(late)
+    def _():
+        pl.semaphore_wait(barrier, ROWS)
+        for s in range(ROWS - 1):
+            greet(0, far_partner(me, s), col)
+        greet(1, me, col)
 
     pair_copy = pltpu.make_async_remote_copy(
         src_ref=surf_v, dst_ref=partner_v, send_sem=pair_sem.at[0], recv_sem=pair_sem.at[1],
@@ -155,9 +162,10 @@
         load_gauss.wait()
         for r in range(LAT):
             weight_v[r : r + 1, :] = jnp.full((1, COLS), gauss_s[r], F32)
-        load_surface.wait()
         load_state.wait()
-        pl.semaphore_wait(barrier, ROWS)
+        @pl.when(jnp.logical_not(late))
+        def _():
+            pl.semaphore_wait(barrier, ROWS)
 
         @pl.when(early)
         def _():
@@ -176,15 +184,12 @@
         def _():
             send_v[me] = own
             out_copy(me).start()
-            greet(1, me, col)
-
-            for s in range(ROWS - 1):
-                greet(0, far_partner(me, s), col)
 
         @pl.when(jnp.logical_not(late))
         def _():
             recv_v[me] = own
 
+        load_surface.wait()
         pair_copy.start()
 
     @pl.when(jnp.logical_not(air))
@@ -313,7 +318,7 @@
                 def _():
                     pair_copy.start()
 
-            for s in range(CHUNK * j // LAT, (CHUNK * (j + 1) - 1) // LAT + 1):
+            for s in range((CHUNK * (j + 1) - 1) // LAT, CHUNK * j // LAT - 1, -1):
                 if s in seen:
                     continue
                 seen.add(s)

time: 33 us -> 32.9 us (level)
  no operation moved by 1% of the time
where the time goes in v5:
time: 32.9 us; the launch traced here: 32.7 us
  Pallas kernels  32.1 us (98%)
  between operations  0.64 us (2%)
    pallas_call x1, Pallas kernels, shards(): pl.pallas_call(kernel, out_shape=(pltpu.VMEM((CELLS, COLS), F32), pltpu.V...  31.2 us
    pallas_call x1, Pallas kernels, shards(): pl.pallas_call(save, out_shape=(pltpu.HBM((CELLS, COLS), F32), pltpu.HBM(...  0.88 us

profile of v5, /device:TPU:1, one launch (start us, length us, event | category | flops | bytes accessed | tf_op | source)
XLA Modules:
  0.0 32.7 jit_solution(14958612939649862749)
XLA Ops:
  0.6 31.2 %shard_map.86 = (f32[1280,128]{1,0:T(8,128)S(1)}, f32[40,128]{1,0:T(8,128)S(1)}) custom-call(f32[1280,128]{1,0:T(8,128)} %bitcast.8, bf16[1280,1280]{1,0:T(8,128)(2,1)} %bitcast.7, f32[40]{0:T(128)} %gauss.1, f32[32,32]{1,0:T(8,128)} %mixing.1, f32[40,128]{1,0:T(8,128)} %bitcast.9, s32[40]{0:T(128)} %bitcast.11, s32[40,128]{1,0:T(8,128)} %bitcast.10), custom_call_target="tpu_custom_call" | custom-call | flops 900000000 | bytes 5000000 | tf_op jit(solution)/shard_map/pallas_call | solution.py:425
  31.8 0.9 %shard_map.87 = (f32[1280,128]{1,0:T(8,128)}, f32[40,128]{1,0:T(8,128)}) custom-call(f32[1280,128]{1,0:T(8,128)S(1)} %get-tuple-element.6.state, f32[40,128]{1,0:T(8,128)S(1)} %get-tuple-element.7.surface), custom_call_target="tpu_custom_call" | custom-call | tf_op jit(solution)/shard_map/pallas_call | solution.py:478
